TPU v7x, 32 devices: a whole 2x2x4 slice. The times are simulated.
32 devices in a mesh: groups: 2 (over y), blk: 4 (over z), narrow: 4 (over x, core).
Axes of the slice: x: 2, y: 2, z: 4, core: 2. Of those that a mesh axis runs over, the one named last changes fastest.
Arguments:
- tokens: bfloat16 [256, 6144], P(('groups', 'blk'), 'narrow'), parts along dimension 0, may hold values from -6 to 6
- skip_flags: int32 [256], P(('groups', 'blk')), parts along dimension 0, may hold values from 0 to 1, as said below
- w_up: bfloat16 [6144, 24576], P('narrow', 'blk'), may hold values from -0.078125 to 0.078125
- w_down: bfloat16 [24576, 6144], P('blk', 'narrow'), may hold values from -0.0390625 to 0.0390625
Outputs:
- update: bfloat16 [256, 6144], P(('groups', 'blk'), 'narrow'), parts along dimension 0
There are 2 independent parts, one for each index of `groups`. A program takes and returns all parts, laid end to end along the dimension named above; an argument that names none is the same for every part. Nothing has to cross between parts.
Inputs may be any that keep to these rules, and one draw needn't show every extreme that they name: `skip_flags`: in each aligned block of 32 tokens at most 24 are active (flag 0), and in every draw some block has exactly 24 active tokens.
All inputs are finite; a program needn't handle non-finite values.
Results may differ from a plain program's by a relative error of at most 0.0049.
Values may be sent and summed in bfloat16 or wider, within the bound.
A program may use at most 128 MiB of HBM per device.

v0:
```python
import jax
import jax.numpy as jnp
from jax import lax
from jax.sharding import PartitionSpec as P


def passed_along(value, axis, steps):
    count = lax.axis_size(axis)
    pairs = [(source, (source + steps) % count) for source in range(count)]
    return lax.ppermute(value, axis, pairs)


def hidden_terms(row_block, w_up, w_down):
    partial_value = jnp.dot(row_block, w_up, preferred_element_type=jnp.float32)
    summed = lax.psum(partial_value, "narrow")
    hidden = jax.nn.gelu(summed, approximate=True).astype(jnp.bfloat16)
    return jnp.dot(hidden, w_down, preferred_element_type=jnp.float32)


def shards(tokens, skip_flags, w_up, w_down):
    active = 1 - skip_flags
    cycle_size = lax.axis_size("blk")
    row_count = tokens.shape[0]
    feature_count = tokens.shape[1]

    def turn_single(turn_index, state_tuple):
        row_block, block_sums = state_tuple
        block_sums = block_sums + hidden_terms(row_block, w_up, w_down)
        row_block = passed_along(row_block, "blk", 1)
        block_sums = passed_along(block_sums, "blk", 1)
        return (row_block, block_sums)

    start_state = (tokens, jnp.zeros((row_count, feature_count), jnp.float32))
    final_state = lax.fori_loop(0, cycle_size, turn_single, start_state)
    running = final_state[1]
    result = running * active[:, None].astype(jnp.float32)
    return result.astype(jnp.bfloat16)


def solution(mesh):
    in_specs = (
        P(("groups", "blk"), "narrow"),
        P(("groups", "blk")),
        P("narrow", "blk"),
        P("blk", "narrow"),
    )
    out_specs = P(("groups", "blk"), "narrow")
    return jax.shard_map(shards, mesh=mesh, in_specs=in_specs, out_specs=out_specs, check_vma=False)
```

profile of v0, /device:TPU:0, one launch (start us, length us, event | category | flops | bytes accessed | tf_op | source)
XLA Modules:
  0.0 267.0 jit_solution(17482225254381903777)
XLA Ops:
  6.5 0.9 copy.17
  7.4 0.0 copy-start
  7.5 252.2 %while.12 = (s32[]{:T(128)}, bf16[32,1536]{1,0:T(8,128)(2,1)S(1)}, f32[32,1536]{1,0:T(8,128)S(1)}, bf16[1536,6144]{1,0:T(8,128)(2,1)}, bf16[6144,1536]{1,0:T(8,128)(2,1)}, /*index=5*/s32[]{:T(128)}) while((s32[]{:T(128)}, bf16[32,1536]{1,0:T(8,128)(2,1)S(1)}, f32[32,1536]{1,0:T(8,128)S(1)}, bf16[1536,6144]{1,0:T(8,128)(2,1)}, ...), condition=%wide.region_2.0_spmd, body=%wide.region_0.0_spmd.sunk | while | flops 1209974784 | bytes 45908156 | solution.py:34
  7.5 0.0 all-reduce.2.cloned.1.call-start
  7.5 10.6 %fusion.30 = f32[32,6144]{1,0:T(8,128)} fusion(bf16[32,1536]{1,0:T(8,128)(2,1)S(1)} %copy.10, bf16[1536,6144]{1,0:T(8,128)(2,1)} %get-tuple-element.89), kind=kOutput, calls=%fused_computation.20.clone.1 | convolution fusion | flops 603979776 | bytes 19759104 | tf_op jit(solution)/shard_map/while/body/eval_jaxpr/dot_general | solution.py:14
  18.1 0.0 all-reduce.2.cloned.1.call-update
  18.2 37.5 %all-reduce.2.cloned.1.call-done = f32[32,6144]{1,0:T(8,128)} async-done(((f32[32,6144]{1,0:T(8,128)}), f32[32,6144]{1,0:T(8,128)}) %all-reduce.2.cloned.1.call-update) | async-done | bytes 786448 | tf_op jit(solution)/shard_map/while/body/eval_jaxpr/psum | solution.py:15
  55.7 8.2 %convolution_add_fusion.2 = f32[32,1536]{1,0:T(8,128)S(1)} fusion(f32[32,1536]{1,0:T(8,128)S(1)} %get-tuple-element.82, bf16[6144,1536]{1,0:T(8,128)(2,1)} %get-tuple-element.90, f32[32,6144]{1,0:T(8,128)} %all-reduce.2.cloned.1.call-done), kind=kOutput, calls=%fused_computation.clone.1 | convolution fusion | flops 605798400 | bytes 20054016 | tf_op jit(solution)/shard_map/while/body/eval_jaxpr/dot_general | solution.py:17
  63.9 1.5 collective-permute-start.1
  65.4 1.5 collective-permute-start
  66.9 6.5 %collective-permute-done = bf16[32,1536]{1,0:T(8,128)(2,1)S(1)} collective-permute-done((bf16[32,1536]{1,0:T(8,128)(2,1)S(1)}, bf16[32,1536]{1,0:T(8,128)(2,1)S(1)}, u32[]{:S(2)}, u32[]{:S(2)}) %collective-permute-start) | collective-permute-done | bytes 98336 | tf_op jit(solution)/shard_map/while/body/eval_jaxpr/ppermute | solution.py:10
  73.4 0.0 collective-permute-done.1
  73.4 0.0 all-reduce.2.cloned.1.call-start
  73.5 10.6 %fusion.30 = f32[32,6144]{1,0:T(8,128)} fusion(bf16[32,1536]{1,0:T(8,128)(2,1)S(1)} %copy.10, bf16[1536,6144]{1,0:T(8,128)(2,1)} %get-tuple-element.89), kind=kOutput, calls=%fused_computation.20.clone.1 | convolution fusion | flops 603979776 | bytes 19759104 | tf_op jit(solution)/shard_map/while/body/eval_jaxpr/dot_general | solution.py:14
  84.1 0.0 all-reduce.2.cloned.1.call-update
  84.1 33.7 %all-reduce.2.cloned.1.call-done = f32[32,6144]{1,0:T(8,128)} async-done(((f32[32,6144]{1,0:T(8,128)}), f32[32,6144]{1,0:T(8,128)}) %all-reduce.2.cloned.1.call-update) | async-done | bytes 786448 | tf_op jit(solution)/shard_map/while/body/eval_jaxpr/psum | solution.py:15
  117.7 8.2 %convolution_add_fusion.2 = f32[32,1536]{1,0:T(8,128)S(1)} fusion(f32[32,1536]{1,0:T(8,128)S(1)} %get-tuple-element.82, bf16[6144,1536]{1,0:T(8,128)(2,1)} %get-tuple-element.90, f32[32,6144]{1,0:T(8,128)} %all-reduce.2.cloned.1.call-done), kind=kOutput, calls=%fused_computation.clone.1 | convolution fusion | flops 605798400 | bytes 20054016 | tf_op jit(solution)/shard_map/while/body/eval_jaxpr/dot_general | solution.py:17
  126.0 1.5 collective-permute-start.1
  127.5 1.5 collective-permute-start
  129.0 6.5 %collective-permute-done = bf16[32,1536]{1,0:T(8,128)(2,1)S(1)} collective-permute-done((bf16[32,1536]{1,0:T(8,128)(2,1)S(1)}, bf16[32,1536]{1,0:T(8,128)(2,1)S(1)}, u32[]{:S(2)}, u32[]{:S(2)}) %collective-permute-start) | collective-permute-done | bytes 98336 | tf_op jit(solution)/shard_map/while/body/eval_jaxpr/ppermute | solution.py:10
  135.5 0.0 collective-permute-done.1
  135.5 0.0 all-reduce.2.cloned.1.call-start
  135.5 10.6 %fusion.30 = f32[32,6144]{1,0:T(8,128)} fusion(bf16[32,1536]{1,0:T(8,128)(2,1)S(1)} %copy.10, bf16[1536,6144]{1,0:T(8,128)(2,1)} %get-tuple-element.89), kind=kOutput, calls=%fused_computation.20.clone.1 | convolution fusion | flops 603979776 | bytes 19759104 | tf_op jit(solution)/shard_map/while/body/eval_jaxpr/dot_general | solution.py:14
  146.2 0.0 all-reduce.2.cloned.1.call-update
  146.2 33.7 %all-reduce.2.cloned.1.call-done = f32[32,6144]{1,0:T(8,128)} async-done(((f32[32,6144]{1,0:T(8,128)}), f32[32,6144]{1,0:T(8,128)}) %all-reduce.2.cloned.1.call-update) | async-done | bytes 786448 | tf_op jit(solution)/shard_map/while/body/eval_jaxpr/psum | solution.py:15
  179.8 8.2 %convolution_add_fusion.2 = f32[32,1536]{1,0:T(8,128)S(1)} fusion(f32[32,1536]{1,0:T(8,128)S(1)} %get-tuple-element.82, bf16[6144,1536]{1,0:T(8,128)(2,1)} %get-tuple-element.90, f32[32,6144]{1,0:T(8,128)} %all-reduce.2.cloned.1.call-done), kind=kOutput, calls=%fused_computation.clone.1 | convolution fusion | flops 605798400 | bytes 20054016 | tf_op jit(solution)/shard_map/while/body/eval_jaxpr/dot_general | solution.py:17
  188.1 1.5 collective-permute-start.1
  189.6 1.5 collective-permute-start
  191.1 6.5 %collective-permute-done = bf16[32,1536]{1,0:T(8,128)(2,1)S(1)} collective-permute-done((bf16[32,1536]{1,0:T(8,128)(2,1)S(1)}, bf16[32,1536]{1,0:T(8,128)(2,1)S(1)}, u32[]{:S(2)}, u32[]{:S(2)}) %collective-permute-start) | collective-permute-done | bytes 98336 | tf_op jit(solution)/shard_map/while/body/eval_jaxpr/ppermute | solution.py:10
  197.6 0.0 collective-permute-done.1
  197.6 0.0 all-reduce.2.cloned.1.call-start
  197.6 10.6 %fusion.30 = f32[32,6144]{1,0:T(8,128)} fusion(bf16[32,1536]{1,0:T(8,128)(2,1)S(1)} %copy.10, bf16[1536,6144]{1,0:T(8,128)(2,1)} %get-tuple-element.89), kind=kOutput, calls=%fused_computation.20.clone.1 | convolution fusion | flops 603979776 | bytes 19759104 | tf_op jit(solution)/shard_map/while/body/eval_jaxpr/dot_general | solution.py:14
  208.2 0.0 all-reduce.2.cloned.1.call-update
  208.3 33.7 %all-reduce.2.cloned.1.call-done = f32[32,6144]{1,0:T(8,128)} async-done(((f32[32,6144]{1,0:T(8,128)}), f32[32,6144]{1,0:T(8,128)}) %all-reduce.2.cloned.1.call-update) | async-done | bytes 786448 | tf_op jit(solution)/shard_map/while/body/eval_jaxpr/psum | solution.py:15
  241.9 8.2 %convolution_add_fusion.2 = f32[32,1536]{1,0:T(8,128)S(1)} fusion(f32[32,1536]{1,0:T(8,128)S(1)} %get-tuple-element.82, bf16[6144,1536]{1,0:T(8,128)(2,1)} %get-tuple-element.90, f32[32,6144]{1,0:T(8,128)} %all-reduce.2.cloned.1.call-done), kind=kOutput, calls=%fused_computation.clone.1 | convolution fusion | flops 605798400 | bytes 20054016 | tf_op jit(solution)/shard_map/while/body/eval_jaxpr/dot_general | solution.py:17
  250.2 1.5 collective-permute-start.1
  251.7 1.5 collective-permute-start
  253.2 6.5 %collective-permute-done = bf16[32,1536]{1,0:T(8,128)(2,1)S(1)} collective-permute-done((bf16[32,1536]{1,0:T(8,128)(2,1)S(1)}, bf16[32,1536]{1,0:T(8,128)(2,1)S(1)}, u32[]{:S(2)}, u32[]{:S(2)}) %collective-permute-start) | collective-permute-done | bytes 98336 | tf_op jit(solution)/shard_map/while/body/eval_jaxpr/ppermute | solution.py:10
  259.7 0.0 collective-permute-done.1
  259.7 0.0 copy-done
  259.7 0.7 multiply_convert_fusion
  (6 shorter events, 0.0 us)
Async XLA Ops:
  7.4 252.3 %copy-start = (s32[32]{0:T(128)S(1)}, s32[32]{0:T(128)}, u32[]{:S(2)}) copy-start(s32[32]{0:T(128)} %param.7) | copy-start | bytes 388
  7.5 48.2 %all-reduce.2.cloned.1.call-start = ((), (), s32[]{:S(2)}) async-start(), calls=%async_computation | async-start | bytes 1572864 | tf_op jit(solution)/shard_map/while/body/eval_jaxpr/psum | solution.py:15
  63.9 9.5 %collective-permute-start.1 = (f32[32,1536]{1,0:T(8,128)S(1)}, f32[32,1536]{1,0:T(8,128)S(1)}, u32[]{:S(2)}, u32[]{:S(2)}) collective-permute-start(f32[32,1536]{1,0:T(8,128)S(1)} %convolution_add_fusion.2), channel_id=1, source_target_pairs={{0,4},{4,8},{8,12},{12,0},{1,5},{5,9},{9,13},{13,1},{2,6},{6,10},{... | collective-permute-start | bytes 589832 | tf_op jit(solution)/shard_map/while/body/eval_jaxpr/ppermute | solution.py:10
  65.4 8.0 %collective-permute-start = (bf16[32,1536]{1,0:T(8,128)(2,1)S(1)}, bf16[32,1536]{1,0:T(8,128)(2,1)S(1)}, u32[]{:S(2)}, u32[]{:S(2)}) collective-permute-start(bf16[32,1536]{1,0:T(8,128)(2,1)S(1)} %copy.10), channel_id=1, source_target_pairs={{0,4},{4,8},{8,12},{12,0},{1,5},{5,9},{9,13},{13,1},{2,6},{6,10},{... | collective-permute-start | bytes 294920 | tf_op jit(solution)/shard_map/while/body/eval_jaxpr/ppermute | solution.py:10
  73.4 44.3 %all-reduce.2.cloned.1.call-start = ((), (), s32[]{:S(2)}) async-start(), calls=%async_computation | async-start | bytes 1572864 | tf_op jit(solution)/shard_map/while/body/eval_jaxpr/psum | solution.py:15
  126.0 9.5 %collective-permute-start.1 = (f32[32,1536]{1,0:T(8,128)S(1)}, f32[32,1536]{1,0:T(8,128)S(1)}, u32[]{:S(2)}, u32[]{:S(2)}) collective-permute-start(f32[32,1536]{1,0:T(8,128)S(1)} %convolution_add_fusion.2), channel_id=1, source_target_pairs={{0,4},{4,8},{8,12},{12,0},{1,5},{5,9},{9,13},{13,1},{2,6},{6,10},{... | collective-permute-start | bytes 589832 | tf_op jit(solution)/shard_map/while/body/eval_jaxpr/ppermute | solution.py:10
  127.5 8.0 %collective-permute-start = (bf16[32,1536]{1,0:T(8,128)(2,1)S(1)}, bf16[32,1536]{1,0:T(8,128)(2,1)S(1)}, u32[]{:S(2)}, u32[]{:S(2)}) collective-permute-start(bf16[32,1536]{1,0:T(8,128)(2,1)S(1)} %copy.10), channel_id=1, source_target_pairs={{0,4},{4,8},{8,12},{12,0},{1,5},{5,9},{9,13},{13,1},{2,6},{6,10},{... | collective-permute-start | bytes 294920 | tf_op jit(solution)/shard_map/while/body/eval_jaxpr/ppermute | solution.py:10
  135.5 44.3 %all-reduce.2.cloned.1.call-start = ((), (), s32[]{:S(2)}) async-start(), calls=%async_computation | async-start | bytes 1572864 | tf_op jit(solution)/shard_map/while/body/eval_jaxpr/psum | solution.py:15
  188.1 9.5 %collective-permute-start.1 = (f32[32,1536]{1,0:T(8,128)S(1)}, f32[32,1536]{1,0:T(8,128)S(1)}, u32[]{:S(2)}, u32[]{:S(2)}) collective-permute-start(f32[32,1536]{1,0:T(8,128)S(1)} %convolution_add_fusion.2), channel_id=1, source_target_pairs={{0,4},{4,8},{8,12},{12,0},{1,5},{5,9},{9,13},{13,1},{2,6},{6,10},{... | collective-permute-start | bytes 589832 | tf_op jit(solution)/shard_map/while/body/eval_jaxpr/ppermute | solution.py:10
  189.6 8.0 %collective-permute-start = (bf16[32,1536]{1,0:T(8,128)(2,1)S(1)}, bf16[32,1536]{1,0:T(8,128)(2,1)S(1)}, u32[]{:S(2)}, u32[]{:S(2)}) collective-permute-start(bf16[32,1536]{1,0:T(8,128)(2,1)S(1)} %copy.10), channel_id=1, source_target_pairs={{0,4},{4,8},{8,12},{12,0},{1,5},{5,9},{9,13},{13,1},{2,6},{6,10},{... | collective-permute-start | bytes 294920 | tf_op jit(solution)/shard_map/while/body/eval_jaxpr/ppermute | solution.py:10
  197.6 44.3 %all-reduce.2.cloned.1.call-start = ((), (), s32[]{:S(2)}) async-start(), calls=%async_computation | async-start | bytes 1572864 | tf_op jit(solution)/shard_map/while/body/eval_jaxpr/psum | solution.py:15
  250.2 9.5 %collective-permute-start.1 = (f32[32,1536]{1,0:T(8,128)S(1)}, f32[32,1536]{1,0:T(8,128)S(1)}, u32[]{:S(2)}, u32[]{:S(2)}) collective-permute-start(f32[32,1536]{1,0:T(8,128)S(1)} %convolution_add_fusion.2), channel_id=1, source_target_pairs={{0,4},{4,8},{8,12},{12,0},{1,5},{5,9},{9,13},{13,1},{2,6},{6,10},{... | collective-permute-start | bytes 589832 | tf_op jit(solution)/shard_map/while/body/eval_jaxpr/ppermute | solution.py:10
  251.7 8.0 %collective-permute-start = (bf16[32,1536]{1,0:T(8,128)(2,1)S(1)}, bf16[32,1536]{1,0:T(8,128)(2,1)S(1)}, u32[]{:S(2)}, u32[]{:S(2)}) collective-permute-start(bf16[32,1536]{1,0:T(8,128)(2,1)S(1)} %copy.10), channel_id=1, source_target_pairs={{0,4},{4,8},{8,12},{12,0},{1,5},{5,9},{9,13},{13,1},{2,6},{6,10},{... | collective-permute-start | bytes 294920 | tf_op jit(solution)/shard_map/while/body/eval_jaxpr/ppermute | solution.py:10
Sparse Core Ops, SparseCore 0:
  18.3 37.3 all-reduce.1
  84.2 33.4 all-reduce.1
  146.3 33.4 all-reduce.1
  208.4 33.4 all-reduce.1
where the time goes:
time: 267 us
  waiting for transfers between devices  165 us (62%)
  matrix products  75.4 us (28%)
  between operations  13.1 us (5%)
  starting transfers between devices  12.2 us (5%)
    psum x4, waiting for transfers between devices, hidden_terms(): summed = lax.psum(partial_value, 'narrow')  138 us
    dot_general x4, matrix products, hidden_terms(): partial_value = jnp.dot(row_block, w_up, preferred_element_type=jnp.float32)  42.4 us
    dot_general x4, matrix products, hidden_terms(): return jnp.dot(hidden, w_down, preferred_element_type=jnp.float32)  32.9 us
    ppermute x8, waiting for transfers between devices, passed_along(): return lax.ppermute(value, axis, pairs)  26 us
    ppermute x8, starting transfers between devices, passed_along(): return lax.ppermute(value, axis, pairs)  12.1 us
  transfers between devices with their start and end apart: 12, of which 8 were waited for; matrix products, arithmetic and copies ran while one was open for 0% of the time, Pallas kernels for 0%

commit v1 on v0

v1 whole, which is shorter than its diff:
```python
import functools
import math

import jax
import jax.numpy as jnp
from jax import lax
from jax.experimental import pallas as pl
from jax.experimental.pallas import tpu as pltpu
from jax.sharding import PartitionSpec as P

CAP = 24
MESH = pl.DeviceIdType.MESH
F32 = jnp.float32
BF16 = jnp.bfloat16


def gelu(v):
    return 0.5 * v * (1.0 + jnp.tanh(math.sqrt(2.0 / math.pi) * (v + 0.044715 * v * v * v)))


def remote(src, dst, send, recv, **where):
    return pltpu.make_async_remote_copy(
        src_ref=src, dst_ref=dst, send_sem=send, recv_sem=recv, device_id=where, device_id_type=MESH
    )


def kernel(
    nz, nn, nk, width,
    flags_ref, tok_ref, wup_hbm, wdn_hbm, out_ref,
    wup, wdn, xg, xs, own, sib_out, sib_in, x_out, x_in, hid, hid_in, acc, y_out, y_in,
    wup_sem, wdn_sem, tok_send, tok_recv, sib_send, sib_recv, x_send, x_recv, hid_send, hid_recv, y_send, y_recv,
):
    rows, dn = tok_ref.shape
    half = dn // 2
    nx = nn // 2
    fh = nk * width
    z = lax.axis_index("blk")
    n = lax.axis_index("narrow")
    core = lax.rem(n, 2)
    sibling = n + 1 - 2 * core
    zpeer = [lax.rem(z + d, nz) for d in range(nz)]
    xpeer = [lax.rem(n + 2 * d, nn) for d in range(nx)]

    def col(k, mine):
        base = core if mine else 1 - core
        return pl.ds(pl.multiple_of(base * fh + k * width, 128), width)

    up_copies, dn_copies = [], []
    for k in range(nk):
        for mine in (0, 1):
            s = 2 * k + mine
            up_copies.append(pltpu.make_async_copy(wup_hbm.at[:, col(k, mine)], wup.at[s], wup_sem.at[s]))
            dn_copies.append(pltpu.make_async_copy(wdn_hbm.at[col(k, mine), :], wdn.at[s], wdn_sem.at[s]))
    for c in up_copies:
        c.start()

    barrier = pltpu.get_barrier_semaphore()
    pl.semaphore_signal(barrier, inc=1, device_id={"narrow": sibling}, device_id_type=MESH)
    for p in xpeer[1:]:
        pl.semaphore_signal(barrier, inc=1, device_id={"narrow": p}, device_id_type=MESH)
    for p in zpeer[1:]:
        pl.semaphore_signal(barrier, inc=1, device_id={"blk": p}, device_id_type=MESH)

    active = (1 - flags_ref[...]).astype(F32)
    upto = (lax.broadcasted_iota(jnp.int32, (rows, rows), 0) <= lax.broadcasted_iota(jnp.int32, (rows, rows), 1))
    rank = jnp.dot(jnp.broadcast_to(active, (8, rows)).astype(BF16), upto.astype(F32).astype(BF16),
                   preferred_element_type=F32)[0:1]
    slot = (lax.broadcasted_iota(jnp.int32, (CAP, rows), 0) + 1).astype(F32)
    pick = (jnp.where(slot == jnp.broadcast_to(rank, (CAP, rows)), 1.0, 0.0)
            * jnp.broadcast_to(active, (CAP, rows))).astype(BF16)
    mine_rows = jnp.dot(pick, tok_ref[...], preferred_element_type=F32)
    xg[z] = jnp.concatenate([mine_rows[:, :half], mine_rows[:, half:]], axis=0).astype(BF16)

    pl.semaphore_wait(barrier, 1 + (nx - 1) + (nz - 1))
    for d in range(1, nz):
        remote(xg.at[z], xg.at[z], tok_send.at[d - 1], tok_recv.at[z], blk=zpeer[d]).start()
    for c in dn_copies:
        c.start()
    for d in range(1, nz):
        j = zpeer[d]
        remote(xg.at[j], xg.at[j], tok_send.at[d - 1], tok_recv.at[j], blk=zpeer[d]).wait_recv()
    left, right = [], []
    for j in range(nz):
        v = xg[j].astype(F32)
        left.append(v[:CAP])
        right.append(v[CAP:])
    xs[:, :half] = jnp.concatenate(left, axis=0).astype(BF16)
    xs[:, half:] = jnp.concatenate(right, axis=0).astype(BF16)

    def sib_copy(k):
        return remote(sib_out.at[k], sib_in.at[k], sib_send.at[k], sib_recv.at[k], narrow=sibling)

    def x_copy(k, d):
        s = k * (nx - 1) + d - 1
        return remote(x_out.at[k], x_in.at[s], x_send.at[s], x_recv.at[s], narrow=xpeer[d])

    def hid_copy(k):
        return remote(hid.at[k], hid_in.at[k], hid_send.at[k], hid_recv.at[k], narrow=sibling)

    def chip_sum(k):
        sib_copy(k).wait_recv()
        total = own[k] + sib_in[k].astype(F32)
        own[k] = total
        x_out[k] = total.astype(BF16)
        for d in range(1, nx):
            x_copy(k, d).start()

    for k in range(nk):
        up_copies[2 * k].wait()
        sib_out[k] = jnp.dot(xs[...], wup[2 * k], preferred_element_type=F32).astype(BF16)
        sib_copy(k).start()
        if k > 0:
            chip_sum(k - 1)
        up_copies[2 * k + 1].wait()
        own[k] = jnp.dot(xs[...], wup[2 * k + 1], preferred_element_type=F32)
    chip_sum(nk - 1)

    for k in range(nk):
        total = own[k]
        for d in range(1, nx):
            x_copy(k, d).wait_recv()
            total = total + x_in[k * (nx - 1) + d - 1].astype(F32)
        hid[k] = gelu(total).astype(BF16)
        hid_copy(k).start()
        dn_copies[2 * k + 1].wait()
        term = jnp.dot(hid[k], wdn[2 * k + 1], preferred_element_type=F32)
        if k == 0:
            acc[...] = term
        else:
            acc[...] += term
        dn_copies[2 * k].wait()
        hid_copy(k).wait_recv()
        acc[...] += jnp.dot(hid_in[k], wdn[2 * k], preferred_element_type=F32)

    for j in range(nz):
        v = acc[CAP * j:CAP * (j + 1), :]
        y_out[j] = jnp.concatenate([v[:, :half], v[:, half:]], axis=0).astype(BF16)

    def y_copy(d):
        return remote(y_out.at[zpeer[d]], y_in.at[d - 1], y_send.at[d - 1], y_recv.at[d - 1], blk=zpeer[d])

    for d in range(1, nz):
        y_copy(d).start()
    mine = acc[pl.ds(pl.multiple_of(z * CAP, 8), CAP), :]
    total = jnp.concatenate([mine[:, :half], mine[:, half:]], axis=0)
    for d in range(1, nz):
        y_copy(d).wait_recv()
        total = total + y_in[d - 1].astype(F32)
    total = jnp.concatenate([total[:CAP], total[CAP:]], axis=1).astype(BF16)
    out_ref[...] = lax.dot_general(
        pick, total, (((0,), (0,)), ((), ())), preferred_element_type=F32
    ).astype(BF16)

    for d in range(1, nz):
        remote(xg.at[z], xg.at[z], tok_send.at[d - 1], tok_recv.at[z], blk=zpeer[d]).wait_send()
        y_copy(d).wait_send()
    for k in range(nk):
        sib_copy(k).wait_send()
        hid_copy(k).wait_send()
        for d in range(1, nx):
            x_copy(k, d).wait_send()


def shards(nz, nn, tokens, skip_flags, w_up, w_down):
    rows, dn = tokens.shape
    ff = w_up.shape[1]
    fh = ff // 2
    width = 512 if fh % 512 == 0 else 128
    nk = fh // width
    nx = nn // 2
    total = CAP * nz
    vmem, dma = pltpu.VMEM, pltpu.SemaphoreType.DMA
    return pl.pallas_call(
        functools.partial(kernel, nz, nn, nk, width),
        out_shape=jax.ShapeDtypeStruct((rows, dn), BF16),
        in_specs=[pl.BlockSpec(memory_space=pltpu.VMEM)] * 2 + [pl.BlockSpec(memory_space=pl.ANY)] * 2,
        out_specs=pl.BlockSpec(memory_space=pltpu.VMEM),
        scratch_shapes=[
            vmem((2 * nk, dn, width), BF16),
            vmem((2 * nk, width, dn), BF16),
            vmem((nz, 2 * CAP, dn // 2), BF16),
            vmem((total, dn), BF16),
            vmem((nk, total, width), F32),
            vmem((nk, total, width), BF16),
            vmem((nk, total, width), BF16),
            vmem((nk, total, width), BF16),
            vmem((nk * (nx - 1), total, width), BF16),
            vmem((nk, total, width), BF16),
            vmem((nk, total, width), BF16),
            vmem((total, dn), F32),
            vmem((nz, 2 * CAP, dn // 2), BF16),
            vmem((nz - 1, 2 * CAP, dn // 2), BF16),
            dma((2 * nk,)), dma((2 * nk,)),
            dma((nz - 1,)), dma((nz,)),
            dma((nk,)), dma((nk,)),
            dma((nk * (nx - 1),)), dma((nk * (nx - 1),)),
            dma((nk,)), dma((nk,)),
            dma((nz - 1,)), dma((nz - 1,)),
        ],
        compiler_params=pltpu.CompilerParams(
            collective_id=0, has_side_effects=True, vmem_limit_bytes=60 * 2 ** 20
        ),
        cost_estimate=pl.CostEstimate(
            flops=4 * total * dn * ff, bytes_accessed=4 * dn * ff, transcendentals=total * fh
        ),
    )(skip_flags.reshape(1, rows), tokens, w_up, w_down)


def solution(mesh):
    in_specs = (
        P(("groups", "blk"), "narrow"),
        P(("groups", "blk")),
        P("narrow", "blk"),
        P("blk", "narrow"),
    )
    out_specs = P(("groups", "blk"), "narrow")
    body = functools.partial(shards, mesh.shape["blk"], mesh.shape["narrow"])
    return jax.shard_map(body, mesh=mesh, in_specs=in_specs, out_specs=out_specs, check_vma=False)
```

time: 267 us -> 40.5 us (0.15)
  waiting for transfers between devices: 165 us -> 0 us
  matrix products: 75.4 us -> 0 us
  Pallas kernels: 0 us -> 38.8 us
  between operations: 13.1 us -> 0.01 us
  starting transfers between devices: 12.2 us -> 0 us
    psum x4 -> x0, waiting for transfers between devices: 138 us -> none  [hidden_terms(): summed = lax.psum(partial_value, 'narrow')]
    dot_general x8 -> x0, matrix products: 75.4 us -> none  [the longest x4 42.4 us: hidden_terms(): partial_value = jnp.dot(row_block, w_up, preferred_element_type=jnp.float32)]
    pallas_call x0 -> x1, Pallas kernels: none -> 38.8 us  [shards(): pl.pallas_call(functools.partial(kernel, nz, nn, nk, width), out_shape=ja...]
    ppermute x8 -> x0, waiting for transfers between devices: 26 us -> none  [passed_along(): return lax.ppermute(value, axis, pairs)]
    ppermute x8 -> x0, starting transfers between devices: 12.1 us -> none  [passed_along(): return lax.ppermute(value, axis, pairs)]
  transfers between devices with their start and end apart: 12 -> 0, of which waited for: 8 -> 0; matrix products, arithmetic and copies ran while one was open for 0% -> 0% of each run, Pallas kernels for 0% -> 0%
where the time goes in v1:
time: 40.5 us; the launch traced here: 40.4 us
  Pallas kernels  38.8 us (96%)
  local copies, waits for them, and re-layouts  1.54 us (4%)
    pallas_call x1, Pallas kernels, shards(): pl.pallas_call(functools.partial(kernel, nz, nn, nk, width), out_shape=ja...  38.8 us
    unnamed x1, local copies, waits for them, and re-layouts  1.54 us

profile of v1, /device:TPU:0, one launch (start us, length us, event | category | flops | bytes accessed | tf_op | source)
XLA Modules:
  0.0 40.4 jit_solution(17105699660313537963)
XLA Ops:
  0.0 38.8 %shard_map.46 = bf16[32,1536]{1,0:T(8,128)(2,1)} custom-call(s32[1,32]{1,0:T(1,128)} %bitcast.1, bf16[32,1536]{1,0:T(8,128)(2,1)} %tok_ref.1, bf16[1536,6144]{1,0:T(8,128)(2,1)} %wup_hbm.1, bf16[6144,1536]{1,0:T(8,128)(2,1)} %wdn_hbm.1), custom_call_target="tpu_custom_call" | custom-call | flops 3623878656 | bytes 37748736 | tf_op jit(solution)/shard_map/pallas_call | solution.py:173
  38.8 1.5 %copy.6 = bf16[32,1536]{1,0:T(8,128)(2,1)} copy(bf16[32,1536]{1,0:T(8,128)(2,1)} %shard_map.46) | data formatting | bytes 196608

commit v2 on v1

v2 whole, which is shorter than its diff:
```python
import functools
import math

import jax
import jax.numpy as jnp
from jax import lax
from jax.experimental import pallas as pl
from jax.experimental.pallas import tpu as pltpu
from jax.sharding import PartitionSpec as P

CAP = 24
MESH = pl.DeviceIdType.MESH
F32 = jnp.float32
BF16 = jnp.bfloat16


def gelu(v):
    return 0.5 * v * (1.0 + jnp.tanh(math.sqrt(2.0 / math.pi) * (v + 0.044715 * v * v * v)))


def remote(src, dst, send, recv, **where):
    return pltpu.make_async_remote_copy(
        src_ref=src, dst_ref=dst, send_sem=send, recv_sem=recv, device_id=where, device_id_type=MESH
    )


def fold(v):
    middle = v.shape[1] // 2
    return jnp.concatenate([v[:, :middle], v[:, middle:]], axis=0)


def unfold(v):
    middle = v.shape[0] // 2
    return jnp.concatenate([v[:middle], v[middle:]], axis=1)


def kernel(
    nz, nn, nk, width, groups,
    flags_ref, tok_ref, wup_hbm, wdn_hbm, out_ref,
    wup, wdn, xg, xs, own, sib_out, sib_in, x_out, x_in, hid, hid_in, acc, y_out, y_in,
    wup_sem, wdn_sem, tok_send, tok_recv, sib_send, sib_recv, x_send, x_recv, hid_send, hid_recv, y_send, y_recv,
):
    rows, dn = tok_ref.shape
    half = dn // 2
    nx = nn // 2
    fh = nk * width
    z = lax.axis_index("blk")
    n = lax.axis_index("narrow")
    core = lax.rem(n, 2)
    sibling = n + 1 - 2 * core
    xpeer = [lax.rem(n + 2 * d, nn) for d in range(nx)]

    order = [z]
    for i in range(1, nz // 2):
        j = lax.rem(z + 2 * i, nz)
        order += [j, j + 1 - 2 * lax.rem(j, 2)]
    order.append(z + 1 - 2 * lax.rem(z, 2))
    ng = len(groups)
    members = CAP * len(groups[0])
    steps = ng * nk

    def col(k, mine):
        base = core if mine else 1 - core
        return pl.ds(pl.multiple_of(base * fh + k * width, 128), width)

    up_copies, dn_copies = [], []
    for k in range(nk):
        for mine in (0, 1):
            s = 2 * k + mine
            up_copies.append(pltpu.make_async_copy(wup_hbm.at[:, col(k, mine)], wup.at[s], wup_sem.at[s]))
            dn_copies.append(pltpu.make_async_copy(wdn_hbm.at[col(k, mine), :], wdn.at[s], wdn_sem.at[s]))
    for c in up_copies:
        c.start()

    barrier = pltpu.get_barrier_semaphore()
    pl.semaphore_signal(barrier, inc=1, device_id={"narrow": sibling}, device_id_type=MESH)
    for p in xpeer[1:]:
        pl.semaphore_signal(barrier, inc=1, device_id={"narrow": p}, device_id_type=MESH)
    for p in order[1:]:
        pl.semaphore_signal(barrier, inc=1, device_id={"blk": p}, device_id_type=MESH)

    active = (1 - flags_ref[...]).astype(F32)
    upto = (lax.broadcasted_iota(jnp.int32, (rows, rows), 0) <= lax.broadcasted_iota(jnp.int32, (rows, rows), 1))
    rank = jnp.dot(jnp.broadcast_to(active, (8, rows)).astype(BF16), upto.astype(F32).astype(BF16),
                   preferred_element_type=F32)[0:1]
    slot = (lax.broadcasted_iota(jnp.int32, (CAP, rows), 0) + 1).astype(F32)
    pick = (jnp.where(slot == jnp.broadcast_to(rank, (CAP, rows)), 1.0, 0.0)
            * jnp.broadcast_to(active, (CAP, rows))).astype(BF16)
    mine_rows = jnp.dot(pick, tok_ref[...], preferred_element_type=F32)
    xg[z] = fold(mine_rows).astype(BF16)

    def tok_copy(p):
        return remote(xg.at[z], xg.at[z], tok_send.at[p], tok_recv.at[z], blk=order[p])

    pl.semaphore_wait(barrier, 1 + (nx - 1) + (nz - 1))
    for p in range(nz - 1, 0, -1):
        tok_copy(p).start()
    for c in dn_copies:
        c.start()

    def sib_copy(s):
        return remote(sib_out.at[s], sib_in.at[s], sib_send.at[s], sib_recv.at[s], narrow=sibling)

    def x_copy(s, d):
        q = s * (nx - 1) + d - 1
        return remote(x_out.at[q], x_in.at[q], x_send.at[q], x_recv.at[q], narrow=xpeer[d])

    def hid_copy(s):
        part = (s % nk, pl.ds(s // nk * members, members))
        return remote(hid.at[part], hid_in.at[part], hid_send.at[s], hid_recv.at[s], narrow=sibling)

    def y_copy(p):
        return remote(y_out.at[p], y_in.at[z], y_send.at[p], y_recv.at[z], blk=order[p])

    def gather(g):
        found = []
        for p in groups[g]:
            j = order[p]
            if p > 0:
                remote(xg.at[j], xg.at[j], tok_send.at[p], tok_recv.at[j], blk=j).wait_recv()
            found.append(unfold(xg[j].astype(F32)))
        xs[g] = jnp.concatenate(found, axis=0).astype(BF16)

    def up(s):
        g, k = divmod(s, nk)
        if k == 0:
            gather(g)
        if g == 0:
            up_copies[2 * k].wait()
        sib_out[s] = jnp.dot(xs[g], wup[2 * k], preferred_element_type=F32).astype(BF16)
        sib_copy(s).start()
        if g == 0:
            up_copies[2 * k + 1].wait()
        own[s] = jnp.dot(xs[g], wup[2 * k + 1], preferred_element_type=F32)

    def chip_sum(s):
        sib_copy(s).wait_recv()
        total = own[s] + sib_in[s].astype(F32)
        own[s] = total
        for d in range(1, nx):
            x_out[s * (nx - 1) + d - 1] = total.astype(BF16)
            x_copy(s, d).start()

    def act(s):
        g, k = divmod(s, nk)
        total = own[s]
        for d in range(1, nx):
            x_copy(s, d).wait_recv()
            total = total + x_in[s * (nx - 1) + d - 1].astype(F32)
        hid[k, g * members:(g + 1) * members] = gelu(total).astype(BF16)
        hid_copy(s).start()

    def down(k):
        dn_copies[2 * k + 1].wait()
        term = jnp.dot(hid[k], wdn[2 * k + 1], preferred_element_type=F32)
        if k == 0:
            acc[...] = term
        else:
            acc[...] += term
        dn_copies[2 * k].wait()
        for g in range(ng):
            hid_copy(g * nk + k).wait_recv()
        acc[...] += jnp.dot(hid_in[k], wdn[2 * k], preferred_element_type=F32)

    lag = nk
    for t in range(steps + lag):
        if t < steps:
            up(t)
        if 1 <= t <= steps:
            chip_sum(t - 1)
        s = t - lag
        if s >= 0:
            act(s)
            if s // nk == ng - 1:
                down(s % nk)

    places = [p for group in groups for p in group]
    for p in range(1, nz):
        i = CAP * places.index(p)
        y_out[p] = fold(acc[i:i + CAP, :]).astype(BF16)
        y_copy(p).start()
    base = CAP * places.index(0)
    total = fold(acc[base:base + CAP, :])
    for p in range(1, nz):
        j = order[p]
        remote(y_out.at[p], y_in.at[j], y_send.at[p], y_recv.at[j], blk=j).wait_recv()
        total = total + y_in[j].astype(F32)
    out_ref[...] = lax.dot_general(
        pick, unfold(total).astype(BF16), (((0,), (0,)), ((), ())), preferred_element_type=F32
    ).astype(BF16)

    for p in range(1, nz):
        tok_copy(p).wait_send()
        y_copy(p).wait_send()
    for s in range(steps):
        sib_copy(s).wait_send()
        hid_copy(s).wait_send()
        for d in range(1, nx):
            x_copy(s, d).wait_send()


def shards(nz, nn, tokens, skip_flags, w_up, w_down):
    rows, dn = tokens.shape
    ff = w_up.shape[1]
    fh = ff // 2
    groups = [[0, nz - 1], list(range(1, nz - 1))] if nz == 4 else [list(range(nz))]
    width = 512 if fh % 512 == 0 else 128
    nk = fh // width
    nx = nn // 2
    total = CAP * nz
    ng = len(groups)
    steps = ng * nk
    members = total // ng
    shape = (members, width)
    vmem, dma = pltpu.VMEM, pltpu.SemaphoreType.DMA
    return pl.pallas_call(
        functools.partial(kernel, nz, nn, nk, width, groups),
        out_shape=jax.ShapeDtypeStruct((rows, dn), BF16),
        in_specs=[pl.BlockSpec(memory_space=pltpu.VMEM)] * 2 + [pl.BlockSpec(memory_space=pl.ANY)] * 2,
        out_specs=pl.BlockSpec(memory_space=pltpu.VMEM),
        scratch_shapes=[
            vmem((2 * nk, dn, width), BF16),
            vmem((2 * nk, width, dn), BF16),
            vmem((nz, 2 * CAP, dn // 2), BF16),
            vmem((ng, members, dn), BF16),
            vmem((steps,) + shape, F32),
            vmem((steps,) + shape, BF16),
            vmem((steps,) + shape, BF16),
            vmem((steps * (nx - 1),) + shape, BF16),
            vmem((steps * (nx - 1),) + shape, BF16),
            vmem((nk, total, width), BF16),
            vmem((nk, total, width), BF16),
            vmem((total, dn), F32),
            vmem((nz, 2 * CAP, dn // 2), BF16),
            vmem((nz, 2 * CAP, dn // 2), BF16),
            dma((2 * nk,)), dma((2 * nk,)),
            dma((nz,)), dma((nz,)),
            dma((steps,)), dma((steps,)),
            dma((steps * (nx - 1),)), dma((steps * (nx - 1),)),
            dma((steps,)), dma((steps,)),
            dma((nz,)), dma((nz,)),
        ],
        compiler_params=pltpu.CompilerParams(
            collective_id=0, has_side_effects=True, vmem_limit_bytes=60 * 2 ** 20
        ),
        cost_estimate=pl.CostEstimate(
            flops=4 * total * dn * ff, bytes_accessed=4 * dn * ff, transcendentals=total * fh
        ),
    )(skip_flags.reshape(1, rows), tokens, w_up, w_down)


def solution(mesh):
    in_specs = (
        P(("groups", "blk"), "narrow"),
        P(("groups", "blk")),
        P("narrow", "blk"),
        P("blk", "narrow"),
    )
    out_specs = P(("groups", "blk"), "narrow")
    body = functools.partial(shards, mesh.shape["blk"], mesh.shape["narrow"])
    return jax.shard_map(body, mesh=mesh, in_specs=in_specs, out_specs=out_specs, check_vma=False)
```

time: 40.5 us -> 39.6 us (0.978)
  Pallas kernels: 38.8 us -> 37.9 us
    pallas_call x1, Pallas kernels: 38.8 us -> 37.9 us  [shards(): pl.pallas_call(functools.partial(kernel, nz, nn, nk, width, groups), out_...]
where the time goes in v2:
time: 39.6 us; the launch traced here: 39.5 us
  Pallas kernels  37.9 us (96%)
  local copies, waits for them, and re-layouts  1.54 us (4%)
    pallas_call x1, Pallas kernels, shards(): pl.pallas_call(functools.partial(kernel, nz, nn, nk, width, groups), out_...  37.9 us
    unnamed x1, local copies, waits for them, and re-layouts  1.54 us

profile of v2, /device:TPU:0, one launch (start us, length us, event | category | flops | bytes accessed | tf_op | source)
XLA Modules:
  0.0 39.5 jit_solution(9926847196181900293)
XLA Ops:
  0.0 37.9 %shard_map.46 = bf16[32,1536]{1,0:T(8,128)(2,1)} custom-call(s32[1,32]{1,0:T(1,128)} %bitcast.1, bf16[32,1536]{1,0:T(8,128)(2,1)} %tok_ref.1, bf16[1536,6144]{1,0:T(8,128)(2,1)} %wup_hbm.1, bf16[6144,1536]{1,0:T(8,128)(2,1)} %wdn_hbm.1), custom_call_target="tpu_custom_call" | custom-call | flops 3623878656 | bytes 37748736 | tf_op jit(solution)/shard_map/pallas_call | solution.py:216
  37.9 1.5 %copy.6 = bf16[32,1536]{1,0:T(8,128)(2,1)} copy(bf16[32,1536]{1,0:T(8,128)(2,1)} %shard_map.46) | data formatting | bytes 196608

commit v3 on v2

--- a/solution.py
+++ b/solution.py
@@ -129,6 +129,8 @@
             up_copies[2 * k].wait()
         sib_out[s] = jnp.dot(xs[g], wup[2 * k], preferred_element_type=F32).astype(BF16)
         sib_copy(s).start()
+        if s > 0:
+            chip_sum(s - 1)
         if g == 0:
             up_copies[2 * k + 1].wait()
         own[s] = jnp.dot(xs[g], wup[2 * k + 1], preferred_element_type=F32)
@@ -166,7 +168,7 @@
     for t in range(steps + lag):
         if t < steps:
             up(t)
-        if 1 <= t <= steps:
+        if t == steps:
             chip_sum(t - 1)
         s = t - lag
         if s >= 0:

time: 39.6 us -> 39.7 us (level)
  no operation moved by 1% of the time
where the time goes in v3:
time: 39.7 us; the launch traced here: 39.6 us
  Pallas kernels  38 us (96%)
  local copies, waits for them, and re-layouts  1.54 us (4%)
    pallas_call x1, Pallas kernels, shards(): pl.pallas_call(functools.partial(kernel, nz, nn, nk, width, groups), out_...  38 us
    unnamed x1, local copies, waits for them, and re-layouts  1.54 us

profile of v3, /device:TPU:0, one launch (start us, length us, event | category | flops | bytes accessed | tf_op | source)
XLA Modules:
  0.0 39.6 jit_solution(11118714882321956336)
XLA Ops:
  0.0 38.0 %shard_map.46 = bf16[32,1536]{1,0:T(8,128)(2,1)} custom-call(s32[1,32]{1,0:T(1,128)} %bitcast.1, bf16[32,1536]{1,0:T(8,128)(2,1)} %tok_ref.1, bf16[1536,6144]{1,0:T(8,128)(2,1)} %wup_hbm.1, bf16[6144,1536]{1,0:T(8,128)(2,1)} %wdn_hbm.1), custom_call_target="tpu_custom_call" | custom-call | flops 3623878656 | bytes 37748736 | tf_op jit(solution)/shard_map/pallas_call | solution.py:218
  38.0 1.5 %copy.6 = bf16[32,1536]{1,0:T(8,128)(2,1)} copy(bf16[32,1536]{1,0:T(8,128)(2,1)} %shard_map.46) | data formatting | bytes 196608
